TPU v7x, 512 devices: a whole 4x4x16 slice. The times are simulated.
512 devices in a mesh: fsdp: 32 (over x_lo, z), side: 16 (over y, x_hi, core).
Axes of the slice: x: 4 (x_hi: 2, x_lo: 2; x = x_hi * 2 + x_lo), y: 4, z: 16, core: 2. Of those that a mesh axis runs over, the one named last changes fastest.
Arguments:
- attn_inputs: bfloat16 [65536, 5120], P(('side', 'fsdp')), may hold values from -24 to 24
- queries: bfloat16 [65536, 2560], P(('side', 'fsdp')), may hold values from -310 to 310
- key_vectors: bfloat16 [65536, 512], P(('side', 'fsdp')), may hold values from -12 to 12
- logp_grad: bfloat16 [65536, 2560], P(('side', 'fsdp')), may hold values from -24 to 24
- new_logp: float32 [65536], P(('side', 'fsdp')), may hold values from -6.5 to -0.01
- old_logp: float32 [65536], P(('side', 'fsdp')), may hold values from -4 to -0.05
- rewards: float32 [32], replicated, may hold values from -8 to 8
- group_ids: int32 [32], replicated, may hold values from 0 to 7
- lengths: int32 [32], replicated, may hold values from 1024 to 2048
- value_proj: bfloat16 [5120, 512], P('fsdp'), may hold values from -0.078125 to 0.078125
- first_moment: bfloat16 [5120, 512], P(('fsdp', 'side')), may hold values from -120 to 120
- second_moment: bfloat16 [5120, 512], P(('fsdp', 'side')), may hold values from 100 to 9984
Outputs:
- input_grad: bfloat16 [65536, 5120], P(('side', 'fsdp'))
- new_proj: bfloat16 [5120, 512], P('fsdp')
- new_first: bfloat16 [5120, 512], P(('fsdp', 'side'))
- new_second: bfloat16 [5120, 512], P(('fsdp', 'side'))
All inputs are finite; a program needn't handle non-finite values.
Results may differ from a plain program's by a relative error of at most 0.03.
Values may be sent and summed in bfloat16 or wider, within the bound.
A program may use at most 64 MiB of HBM per device.

v0:
```python
import math
import jax
import jax.numpy as jnp
from jax import lax
from jax.sharding import Mesh
from jax.sharding import PartitionSpec as P

QH = 20
KVH = 4
HEAD = 128
ROLLS = 2
FSDP = ("fsdp_0", "fsdp_1")
SIDE_FSDP = ("side", "fsdp_0", "fsdp_1")
FSDP_SIDE = ("fsdp_0", "fsdp_1", "side")
clip_low = 0.8
clip_high = 1.2
decay_first = 0.9
decay_second = 0.95
step_rate = 0.001
weight_decay = 0.1
adam_eps = 1e-08
bias_first = 1.0 - 0.9**10
bias_second = 1.0 - 0.95**10


def laid_out(pieces, dim):
    pieces = jnp.moveaxis(pieces, 0, dim)
    dims = pieces.shape
    return pieces.reshape(*dims[:dim], dims[dim] * dims[dim + 1], *dims[dim + 2 :])


def all_blocks(value, axes, sequence):
    pieces = value
    for k in sequence:
        pieces = lax.all_gather(pieces, axes[k])
    done = sequence[::-1]
    back = [done.index(k) for k in range(len(axes))]
    pieces = pieces.transpose(*back, *range(len(axes), pieces.ndim))
    return pieces.reshape(-1, *value.shape)


def whole_of(value, axes, sequence, dim):
    return laid_out(all_blocks(value, axes, sequence), dim)


def reduced_to_own(pieces, axes, sequence):
    dims = [lax.axis_size(a) for a in axes]
    pieces = pieces.reshape(*dims, *pieces.shape[1:])
    pieces = pieces.transpose(*sequence, *range(len(axes), pieces.ndim))
    pieces = pieces.reshape(-1, *pieces.shape[len(axes) :])
    for k in sequence:
        pieces = lax.psum_scatter(pieces, axes[k], scatter_dimension=0, tiled=True)
    return pieces[0]


def split_up(value, dim, peers):
    before, after = (value.shape[:dim], value.shape[dim + 1 :])
    return jnp.moveaxis(value.reshape(*before, peers, -1, *after), dim, 0)


def summed_rows(value, axes, sequence, dim):
    peers = lax.axis_size(axes)
    return reduced_to_own(split_up(value, dim, peers), axes, sequence)


def sum_at_owner(value, axis, dim):
    pieces = split_up(value, dim, lax.axis_size(axis))
    arrived = lax.all_to_all(pieces, axis, split_axis=0, concat_axis=0, tiled=True)
    return arrived.astype(jnp.float32).sum(axis=0)


def from_everyone(value, axis):
    peers = lax.axis_size(axis)
    return lax.all_to_all(
        jnp.broadcast_to(value[None], (peers, *value.shape)), axis, 0, 0, tiled=True
    )


def collect(value, axis, dim):
    pieces = from_everyone(value, axis)
    return laid_out(pieces, dim)


def advantages(rewards, group_ids):
    group_count = rewards.shape[0] // 4
    member = (group_ids[:, None] == jnp.arange(group_count, dtype=jnp.int32)[None, :]).astype(
        jnp.float32
    )
    counts = jnp.maximum(jnp.sum(member, axis=0), 1.0)
    group_mean = jnp.sum(member * rewards[:, None], axis=0) / counts
    own_mean = jnp.sum(member * group_mean[None, :], axis=1)
    spread = rewards - own_mean
    variance = jnp.sum(member * (spread * spread)[:, None], axis=0) / counts
    own_std = jnp.sqrt(jnp.sum(member * variance[None, :], axis=1))
    return spread / jnp.maximum(own_std, 1.0)


def coefficient(new_lp, old_lp, adv_tok, len_tok, pos_tok, full_len):
    ratio_now = jnp.exp(new_lp - old_lp)
    clipped = jnp.clip(ratio_now, clip_low, clip_high)
    active = (ratio_now * adv_tok <= clipped * adv_tok) & (pos_tok < len_tok)
    len_weight = full_len / len_tok.astype(jnp.float32)
    return jnp.where(active, -adv_tok * ratio_now * len_weight, 0.0)


def block_values(query_blk, grad_blk, roll_keys, first_pos):
    tok_rows = query_blk.shape[0]
    key_count = roll_keys.shape[0]
    per_group = QH // KVH
    score_scale = 1.0 / math.sqrt(HEAD)
    query_pos = first_pos + jnp.arange(tok_rows, dtype=jnp.int32)
    key_pos = jnp.arange(key_count, dtype=jnp.int32)
    allowed = jnp.tile(key_pos[None, :] <= query_pos[:, None], (per_group, 1))
    pieces = []
    for kv_head in range(KVH):
        col_low = kv_head * per_group * HEAD
        col_high = col_low + per_group * HEAD
        q_part = (
            query_blk[:, col_low:col_high]
            .reshape(tok_rows, per_group, HEAD)
            .transpose(1, 0, 2)
            .reshape(per_group * tok_rows, HEAD)
        )
        g_part = (
            grad_blk[:, col_low:col_high]
            .reshape(tok_rows, per_group, HEAD)
            .transpose(1, 0, 2)
            .reshape(per_group * tok_rows, HEAD)
        )
        k_part = roll_keys[:, kv_head * HEAD : (kv_head + 1) * HEAD]
        scores = jnp.dot(q_part, k_part.T, preferred_element_type=jnp.float32) * score_scale
        scores = jnp.where(allowed, scores, -1e30)
        top_val = jnp.max(scores, axis=1, keepdims=True)
        expo = jnp.exp(scores - top_val)
        attention = (expo / jnp.sum(expo, axis=1, keepdims=True)).astype(jnp.bfloat16)
        pieces.append(jnp.dot(attention.T, g_part, preferred_element_type=jnp.float32))
    return jnp.concatenate(pieces, axis=1)


def adam_rows(old_rows, grad_rows, first_moment, second_moment):
    first = decay_first * first_moment.astype(jnp.float32) + (1.0 - decay_first) * grad_rows
    second = (
        decay_second * second_moment.astype(jnp.float32)
        + (1.0 - decay_second) * grad_rows * grad_rows
    )
    weight_now = old_rows.astype(jnp.float32)
    update = (
        first / bias_first / (jnp.sqrt(second / bias_second) + adam_eps) + weight_decay * weight_now
    )
    return (
        (weight_now - step_rate * update).astype(jnp.bfloat16),
        first.astype(jnp.bfloat16),
        second.astype(jnp.bfloat16),
    )


def shards(
    attn_inputs,
    queries,
    key_vectors,
    logp_grad,
    new_logp,
    old_logp,
    rewards,
    group_ids,
    lengths,
    value_proj,
    first_moment,
    second_moment,
):
    fsdp_size = lax.axis_size(FSDP)
    fsdp_index = lax.axis_index(FSDP)
    side_index = lax.axis_index("side")
    tok_rows = attn_inputs.shape[0]
    half = tok_rows // ROLLS
    full_len = half * fsdp_size
    width = key_vectors.shape[1]
    first_pos = fsdp_index * half
    advantage = advantages(rewards, group_ids)
    slot = jnp.arange(tok_rows, dtype=jnp.int32)
    global_roll = side_index * ROLLS + slot // half
    position = first_pos + slot % half
    coeff = coefficient(
        new_logp, old_logp, advantage[global_roll], lengths[global_roll], position, full_len
    )
    out_grad = (coeff[:, None] * logp_grad.astype(jnp.float32)).astype(jnp.bfloat16)
    in_columns = lax.all_to_all(attn_inputs, FSDP, split_axis=1, concat_axis=0, tiled=True)
    all_keys = whole_of(key_vectors, FSDP, (0, 1), 0)
    keys_split = all_keys.reshape(fsdp_size, ROLLS, half, width)
    partials = []
    for roll in range(ROLLS):
        roll_keys = keys_split[:, roll].reshape(full_len, width)
        partials.append(
            block_values(
                queries[roll * half : (roll + 1) * half],
                out_grad[roll * half : (roll + 1) * half],
                roll_keys,
                first_pos,
            )
        )
    stacked = jnp.stack(partials, axis=0)
    placed = (
        stacked.reshape(ROLLS, fsdp_size, half, width)
        .transpose(1, 0, 2, 3)
        .reshape(fsdp_size * tok_rows, width)
    )
    own_grad = (
        summed_rows(placed.astype(jnp.bfloat16), FSDP, (1, 0), 0)
        .astype(jnp.float32)
        .astype(jnp.bfloat16)
    )
    values_grad = lax.all_gather(own_grad, FSDP, axis=0, tiled=True)
    grad_cols = jnp.dot(values_grad, value_proj.T, preferred_element_type=jnp.float32).astype(
        jnp.bfloat16
    )
    input_grad = lax.all_to_all(grad_cols, FSDP, split_axis=0, concat_axis=1, tiled=True)
    weight_grad = lax.dot_general(
        in_columns, values_grad, (((0,), (0,)), ((), ())), preferred_element_type=jnp.float32
    )
    shard_grad = sum_at_owner(weight_grad.astype(jnp.bfloat16), "side", 0)
    shard_rows = shard_grad.shape[0]
    old_rows = lax.dynamic_slice_in_dim(value_proj, side_index * shard_rows, shard_rows, 0)
    new_rows, new_first, new_second = adam_rows(old_rows, shard_grad, first_moment, second_moment)
    new_proj = collect(new_rows, "side", 0)
    return (input_grad, new_proj, new_first, new_second)


def solution(mesh):
    torus = Mesh(mesh.devices.reshape(2, 16, mesh.shape["side"]), ("fsdp_0", "fsdp_1", "side"))
    placed = (
        P(SIDE_FSDP, None),
        P(SIDE_FSDP, None),
        P(SIDE_FSDP, None),
        P(SIDE_FSDP, None),
        P(SIDE_FSDP),
        P(SIDE_FSDP),
        P(),
        P(),
        P(),
        P(FSDP, None),
        P(FSDP_SIDE, None),
        P(FSDP_SIDE, None),
    )
    return jax.shard_map(
        shards,
        mesh=torus,
        in_specs=placed,
        out_specs=(P(SIDE_FSDP, None), P(FSDP, None), P(FSDP_SIDE, None), P(FSDP_SIDE, None)),
        check_vma=False,
    )
```

profile of v0, /device:TPU:32, one launch (start us, length us, event | category | flops | bytes accessed | tf_op | source)
XLA Modules:
  0.0 514.3 jit_solution(6397335464819392959)
XLA Ops:
  7.3 7.6 %all-gather = bf16[256,512]{1,0:T(8,128)(2,1)} all-gather(bf16[128,512]{1,0:T(8,128)(2,1)} %param.14), channel_id=2, replica_groups=mesh['fsdp_0'=2,'fsdp_1'=16,'side'=16] {'fsdp_0'}, dimensions={0}, use_global_device_ids=true | all-gather | bytes 393216 | tf_op jit(solution)/shard_map/all_gather | solution.py:35
  15.0 1.2 fusion.53
  20.2 1.2 gather_fusion
  30.1 67.4 %all-gather.6.cloned.1.call-done = bf16[32,128,512]{2,1,0:T(8,128)(2,1)} async-done(((bf16[2,128,512]{2,1,0:T(8,128)(2,1)}), bf16[32,128,512]{2,1,0:T(8,128)(2,1)}) %all-gather.6.cloned.1.call-update) | async-done | bytes 4194320 | tf_op jit(solution)/shard_map/all_gather | solution.py:35
  97.5 2.6 copy.92
  109.8 1.5 pad_maximum_fusion
  111.3 3.9 copy.100
  124.5 2.6 copy.109
  127.1 2.6 maximum_bitcast_fusion
  130.2 2.4 copy.111
  132.6 75.9 %reduce-scatter.3.cloned.1.call-done = bf16[2,128,512]{2,1,0:T(8,128)(2,1)} async-done(((bf16[32,128,512]{2,1,0:T(8,128)(2,1)}), bf16[2,128,512]{2,1,0:T(8,128)(2,1)}) %reduce-scatter.3.cloned.1.call-update) | async-done | bytes 262160 | tf_op jit(solution)/shard_map/reduce_scatter | solution.py:52
  208.6 23.0 %reduce-scatter.5.cloned.1.call-done = bf16[1,128,512]{2,1,0:T(8,128)(2,1)} async-done(((bf16[2,128,512]{2,1,0:T(8,128)(2,1)}), bf16[1,128,512]{2,1,0:T(8,128)(2,1)}) %reduce-scatter.5.cloned.1.call-update) | async-done | bytes 131088 | tf_op jit(solution)/shard_map/reduce_scatter | solution.py:52
  232.4 91.0 %all_to_all.48 = bf16[128,32,160]{0,2,1:T(8,128)(2,1)S(1)} all-to-all(bf16[128,32,160]{0,2,1:T(8,128)(2,1)S(1)} %bitcast.123), channel_id=1, replica_groups=mesh['fsdp_0'=2,'fsdp_1'=16,'side'=16] {'fsdp_0','fsdp_1'}, dimensions={1} | all-to-all | bytes 2621440 | tf_op jit(solution)/shard_map/all_to_all | solution.py:187
  323.4 77.8 %all-gather.8.cloned.1.call-done = bf16[1,4096,512]{2,1,0:T(8,128)(2,1)} async-done(((bf16[1,128,512]{2,1,0:T(8,128)(2,1)}), bf16[1,4096,512]{2,1,0:T(8,128)(2,1)}) %all-gather.8.cloned.1.call-update) | async-done | bytes 4194320 | tf_op jit(solution)/shard_map/all_gather | solution.py:212
  401.2 3.0 fusion.29
  405.0 6.4 %all-to-all-start.2 = ((bf16[16,10,512]{2,1,0:T(8,128)(2,1)}), bf16[16,10,512]{2,1,0:T(8,128)(2,1)S(1)}, u32[]{:S(2)}, u32[]{:S(2)}) async-start(bf16[16,10,512]{2,1,0:T(8,128)(2,1)} %reshape.265), calls=%async_computation.4 | async-start | bytes 524288 | tf_op jit(solution)/shard_map/all_to_all | solution.py:68
  411.4 9.6 %all-to-all-done.2 = bf16[16,10,512]{2,1,0:T(8,128)(2,1)S(1)} async-done(((bf16[16,10,512]{2,1,0:T(8,128)(2,1)}), bf16[16,10,512]{2,1,0:T(8,128)(2,1)S(1)}, u32[]{:S(2)}, u32[]{:S(2)}) %all-to-all-start.2) | async-done | bytes 163872 | tf_op jit(solution)/shard_map/all_to_all | solution.py:68
  422.4 3.5 all-to-all-start.3
  426.0 3.7 fusion.19
  429.7 1.3 copy.127
  430.9 4.5 all-to-all-done.3
  435.5 6.1 %all-to-all-start = ((bf16[32,128,160]{1,2,0:T(8,128)(2,1)}), bf16[32,128,160]{1,2,0:T(8,128)(2,1)S(1)}, u32[]{:S(2)}, u32[]{:S(2)}) async-start(bf16[32,128,160]{1,2,0:T(8,128)(2,1)} %bitcast.100), calls=%async_computation.2 | async-start | bytes 2621440 | tf_op jit(solution)/shard_map/all_to_all | solution.py:216
  442.3 64.1 %all-to-all-done = bf16[32,128,160]{1,2,0:T(8,128)(2,1)S(1)} async-done(((bf16[32,128,160]{1,2,0:T(8,128)(2,1)}), bf16[32,128,160]{1,2,0:T(8,128)(2,1)S(1)}, u32[]{:S(2)}, u32[]{:S(2)}) %all-to-all-start) | async-done | bytes 1310752 | tf_op jit(solution)/shard_map/all_to_all | solution.py:216
  506.3 1.4 copy.115
  (124 shorter events, 35.7 us)
Async XLA Ops:
  7.2 14.2 %copy-start = (s32[32]{0:T(128)S(1)}, s32[32]{0:T(128)}, u32[]{:S(2)}) copy-start(s32[32]{0:T(128)} %param.20) | copy-start | bytes 388
  7.2 15.5 %copy-start.15 = (f32[128]{0:T(128)S(1)}, f32[128]{0:T(128)}, u32[]{:S(2)}) copy-start(f32[128]{0:T(128)} %param.16) | copy-start | bytes 1540
  7.2 15.5 %copy-start.16 = (f32[128]{0:T(128)S(1)}, f32[128]{0:T(128)}, u32[]{:S(2)}) copy-start(f32[128]{0:T(128)} %param.17) | copy-start | bytes 1540
  7.2 15.5 %copy-start.3 = (bf16[128,2560]{1,0:T(8,128)(2,1)S(1)}, bf16[128,2560]{1,0:T(8,128)(2,1)}, u32[]{:S(2)}) copy-start(bf16[128,2560]{1,0:T(8,128)(2,1)} %param.15) | copy-start | bytes 1966084
  7.2 90.3 %all-gather.6.cloned.1.call-start = ((), (), s32[]{:S(2)}) async-start(), calls=%async_computation.8 | async-start | bytes 4456448 | tf_op jit(solution)/shard_map/all_gather | solution.py:35
  14.9 193.6 %reduce-scatter.3.cloned.1.call-start = ((), (), s32[]{:S(2)}) async-start(), calls=%async_computation.6 | async-start | bytes 4456448 | tf_op jit(solution)/shard_map/reduce_scatter | solution.py:52
  102.9 1.3 copy-start.9
  104.9 0.9 copy-start.10
  106.6 0.9 copy-start.11
  108.2 0.9 copy-start.12
  117.4 1.2 copy-start.5
  119.4 0.9 copy-start.6
  121.0 0.9 copy-start.7
  122.7 0.9 copy-start.8
  132.6 99.1 %copy-start.2 = (bf16[128,5120]{1,0:T(8,128)(2,1)S(1)}, bf16[128,5120]{1,0:T(8,128)(2,1)}, u32[]{:S(2)}) copy-start(bf16[128,5120]{1,0:T(8,128)(2,1)} %param.12) | copy-start | bytes 3932164
  132.6 99.0 %reduce-scatter.5.cloned.1.call-start = ((), (), s32[]{:S(2)}) async-start(), calls=%async_computation.7 | async-start | bytes 393216 | tf_op jit(solution)/shard_map/reduce_scatter | solution.py:52
  208.5 192.7 %all-gather.8.cloned.1.call-start = ((), (), s32[]{:S(2)}) async-start(), calls=%async_computation.9 | async-start | bytes 4325376 | tf_op jit(solution)/shard_map/all_gather | solution.py:212
  323.4 97.6 %copy-start.4 = (bf16[160,512]{1,0:T(8,128)(2,1)S(1)}, bf16[160,512]{1,0:T(8,128)(2,1)}, u32[]{:S(2)}) copy-start(bf16[160,512]{1,0:T(8,128)(2,1)} %param.21) | copy-start | bytes 491524
  323.4 97.6 %copy-start.13 = (bf16[10,512]{1,0:T(8,128)(2,1)S(1)}, bf16[10,512]{1,0:T(8,128)(2,1)}, u32[]{:S(2)}) copy-start(bf16[10,512]{1,0:T(8,128)(2,1)} %param.23) | copy-start | bytes 30724
  323.4 97.6 %copy-start.14 = (bf16[10,512]{1,0:T(8,128)(2,1)S(1)}, bf16[10,512]{1,0:T(8,128)(2,1)}, u32[]{:S(2)}) copy-start(bf16[10,512]{1,0:T(8,128)(2,1)} %param.22) | copy-start | bytes 30724
  405.0 16.0 %all-to-all-start.2 = ((bf16[16,10,512]{2,1,0:T(8,128)(2,1)}), bf16[16,10,512]{2,1,0:T(8,128)(2,1)S(1)}, u32[]{:S(2)}, u32[]{:S(2)}) async-start(bf16[16,10,512]{2,1,0:T(8,128)(2,1)} %reshape.265), calls=%async_computation.4 | async-start | bytes 524288 | tf_op jit(solution)/shard_map/all_to_all | solution.py:68
  422.4 13.1 %all-to-all-start.3 = ((bf16[16,10,512]{2,1,0:T(8,128)(2,1)}), bf16[16,10,512]{2,1,0:T(8,128)(2,1)S(1)}, u32[]{:S(2)}, u32[]{:S(2)}) async-start(bf16[16,10,512]{2,1,0:T(8,128)(2,1)} %broadcast_in_dim.19), calls=%async_computation.5 | async-start | bytes 524288 | tf_op jit(solution)/shard_map/all_to_all | solution.py:74
  435.5 72.3 %copy-start.1 = (s32[32]{0:T(128)S(1)}, s32[32]{0:T(128)}, u32[]{:S(2)}) copy-start(s32[32]{0:T(128)} %param.20) | copy-start | bytes 388
  435.5 70.9 %all-to-all-start = ((bf16[32,128,160]{1,2,0:T(8,128)(2,1)}), bf16[32,128,160]{1,2,0:T(8,128)(2,1)S(1)}, u32[]{:S(2)}, u32[]{:S(2)}) async-start(bf16[32,128,160]{1,2,0:T(8,128)(2,1)} %bitcast.100), calls=%async_computation.2 | async-start | bytes 2621440 | tf_op jit(solution)/shard_map/all_to_all | solution.py:216
Sparse Core Ops, SparseCore 0:
  15.0 82.4 all-gather.5
  132.7 75.7 reduce-scatter.2
  211.3 20.2 reduce-scatter.4
  233.7 167.3 all-gather.7
where the time goes:
time: 515 us; the launch traced here: 514 us
  waiting for transfers between devices  322 us (63%)
  blocking collectives  98.6 us (19%)
  local copies, waits for them, and re-layouts  31.3 us (6%)
  matrix products  18.5 us (4%)
  starting transfers between devices  16.2 us (3%)
  between operations  14.3 us (3%)
  other arithmetic  13.2 us (3%)
    reduce_scatter x2, waiting for transfers between devices, reduced_to_own(): pieces = lax.psum_scatter(pieces, axes[k], scatter_dimension=0, tiled=True)  98.9 us
    all_to_all x1, blocking collectives, shards(): lax.all_to_all(attn_inputs, FSDP, split_axis=1, concat_axis=0, tiled=True)  91 us
    all_gather x1, waiting for transfers between devices, shards(): values_grad = lax.all_gather(own_grad, FSDP, axis=0, tiled=True)  77.8 us
    all_gather x1, waiting for transfers between devices, all_blocks(): pieces = lax.all_gather(pieces, axes[k])  67.4 us
    all_to_all x1, waiting for transfers between devices, shards(): lax.all_to_all(grad_cols, FSDP, split_axis=0, concat_axis=1, tiled=True)  64.1 us
  transfers between devices with their start and end apart: 7, of which 7 were waited for; matrix products, arithmetic and copies ran while one was open for 4% of the time, Pallas kernels for 0%

commit v1 on v0

--- a/solution.py
+++ b/solution.py
@@ -209,7 +209,9 @@
         .astype(jnp.float32)
         .astype(jnp.bfloat16)
     )
-    values_grad = lax.all_gather(own_grad, FSDP, axis=0, tiled=True)
+    values_grad = jnp.concatenate(
+        lax.all_to_all(jnp.stack([own_grad] * lax.axis_size(FSDP)), FSDP, 0, 0), axis=0
+    )
     grad_cols = jnp.dot(values_grad, value_proj.T, preferred_element_type=jnp.float32).astype(
         jnp.bfloat16
     )

time: 515 us -> 587 us (1.14)
  blocking collectives: 98.6 us -> 210 us
  waiting for transfers between devices: 322 us -> 272 us
  starting transfers between devices: 16.2 us -> 24 us
    all_to_all x1, blocking collectives: 91 us -> 202 us  [shards(): lax.all_to_all(jnp.stack([own_grad] * lax.axis_size(FSDP)), FSDP, 0, 0)]
    all_gather x1 -> x0, waiting for transfers between devices: 77.8 us -> none  [shards(): values_grad = lax.all_gather(own_grad, FSDP, axis=0, tiled=True)]
    reduce_scatter x2, waiting for transfers between devices: 98.9 us -> 127 us  [reduced_to_own(): pieces = lax.psum_scatter(pieces, axes[k], scatter_dimension=0, tiled=True)]
    all_to_all x0 -> x1, starting transfers between devices: none -> 9.01 us  [shards(): lax.all_to_all(attn_inputs, FSDP, split_axis=1, concat_axis=0, tiled=True)]
  transfers between devices with their start and end apart: 7 -> 7, of which waited for: 7 -> 6; matrix products, arithmetic and copies ran while one was open for 4% -> 4% of each run, Pallas kernels for 0% -> 0%
where the time goes in v1:
time: 587 us; the launch traced here: 586 us
  waiting for transfers between devices  272 us (46%)
  blocking collectives  210 us (36%)
  local copies, waits for them, and re-layouts  36.5 us (6%)
  starting transfers between devices  24 us (4%)
  matrix products  16.3 us (3%)
  between operations  14.3 us (2%)
  other arithmetic  13.2 us (2%)
    all_to_all x1, blocking collectives, shards(): lax.all_to_all(jnp.stack([own_grad] * lax.axis_size(FSDP)), FSDP, 0, 0)  202 us
    reduce_scatter x2, waiting for transfers between devices, reduced_to_own(): pieces = lax.psum_scatter(pieces, axes[k], scatter_dimension=0, tiled=True)  127 us
    all_gather x1, waiting for transfers between devices, all_blocks(): pieces = lax.all_gather(pieces, axes[k])  67.4 us
    all_to_all x1, waiting for transfers between devices, shards(): lax.all_to_all(grad_cols, FSDP, split_axis=0, concat_axis=1, tiled=True)  64.1 us
  transfers between devices with their start and end apart: 7, of which 6 were waited for; matrix products, arithmetic and copies ran while one was open for 4% of the time, Pallas kernels for 0%

profile of v1, /device:TPU:32, one launch (start us, length us, event | category | flops | bytes accessed | tf_op | source)
XLA Modules:
  0.0 586.2 jit_solution(11390144644669981370)
XLA Ops:
  7.3 7.6 %all-gather = bf16[256,512]{1,0:T(8,128)(2,1)} all-gather(bf16[128,512]{1,0:T(8,128)(2,1)} %param.14), channel_id=2, replica_groups=mesh['fsdp_0'=2,'fsdp_1'=16,'side'=16] {'fsdp_0'}, dimensions={0}, use_global_device_ids=true | all-gather | bytes 393216 | tf_op jit(solution)/shard_map/all_gather | solution.py:35
  30.1 67.4 %all-gather.4.cloned.1.call-done = bf16[32,128,512]{2,1,0:T(8,128)(2,1)} async-done(((bf16[2,128,512]{2,1,0:T(8,128)(2,1)}), bf16[32,128,512]{2,1,0:T(8,128)(2,1)}) %all-gather.4.cloned.1.call-update) | async-done | bytes 4194320 | tf_op jit(solution)/shard_map/all_gather | solution.py:35
  97.5 2.6 copy.89
  109.8 1.5 pad_maximum_fusion
  111.3 3.9 copy.97
  124.5 2.6 copy.106
  127.1 2.6 maximum_bitcast_fusion
  130.2 2.4 copy.108
  132.6 1.3 copy-done.3
  133.9 1.4 copy.110
  135.3 9.0 %all-to-all-start.2 = ((bf16[128,32,160]{0,2,1:T(8,128)(2,1)}), bf16[128,32,160]{0,2,1:T(8,128)(2,1)S(1)}, u32[]{:S(2)}, u32[]{:S(2)}) async-start(bf16[128,32,160]{0,2,1:T(8,128)(2,1)} %bitcast.50), calls=%async_computation.4 | async-start | bytes 2621440 | tf_op jit(solution)/shard_map/all_to_all | solution.py:187
  144.4 102.8 %reduce-scatter.3.cloned.1.call-done = bf16[2,128,512]{2,1,0:T(8,128)(2,1)} async-done(((bf16[32,128,512]{2,1,0:T(8,128)(2,1)}), bf16[2,128,512]{2,1,0:T(8,128)(2,1)}) %reduce-scatter.3.cloned.1.call-update) | async-done | bytes 262160 | tf_op jit(solution)/shard_map/reduce_scatter | solution.py:52
  247.2 24.0 %reduce-scatter.5.cloned.1.call-done = bf16[1,128,512]{2,1,0:T(8,128)(2,1)} async-done(((bf16[2,128,512]{2,1,0:T(8,128)(2,1)}), bf16[1,128,512]{2,1,0:T(8,128)(2,1)}) %reduce-scatter.5.cloned.1.call-update) | async-done | bytes 131088 | tf_op jit(solution)/shard_map/reduce_scatter | solution.py:52
  271.2 1.4 stack.14
  272.6 201.9 %all_to_all.50 = bf16[32,128,512]{2,1,0:T(8,128)(2,1)S(1)} all-to-all(bf16[32,128,512]{2,1,0:T(8,128)(2,1)S(1)} %stack.14), channel_id=1, replica_groups=mesh['fsdp_0'=2,'fsdp_1'=16,'side'=16] {'fsdp_0','fsdp_1'}, dimensions={0} | all-to-all | bytes 8388608 | tf_op jit(solution)/shard_map/all_to_all | solution.py:213
  474.5 1.9 copy-done.2
  478.0 6.8 %all-to-all-start.3 = ((bf16[16,10,512]{2,1,0:T(8,128)(2,1)}), bf16[16,10,512]{2,1,0:T(8,128)(2,1)S(1)}, u32[]{:S(2)}, u32[]{:S(2)}) async-start(bf16[16,10,512]{2,1,0:T(8,128)(2,1)} %reshape.271), calls=%async_computation.5 | async-start | bytes 524288 | tf_op jit(solution)/shard_map/all_to_all | solution.py:68
  484.8 9.6 %all-to-all-done.3 = bf16[16,10,512]{2,1,0:T(8,128)(2,1)S(1)} async-done(((bf16[16,10,512]{2,1,0:T(8,128)(2,1)}), bf16[16,10,512]{2,1,0:T(8,128)(2,1)S(1)}, u32[]{:S(2)}, u32[]{:S(2)}) %all-to-all-start.3) | async-done | bytes 163872 | tf_op jit(solution)/shard_map/all_to_all | solution.py:68
  495.8 3.5 all-to-all-start.4
  499.4 3.7 fusion.16
  504.4 4.5 all-to-all-done.4
  508.9 4.5 all-to-all-start.1
  514.1 64.1 %all-to-all-done.1 = bf16[32,128,160]{1,2,0:T(8,128)(2,1)S(1)} async-done(((bf16[32,128,160]{1,2,0:T(8,128)(2,1)}), bf16[32,128,160]{1,2,0:T(8,128)(2,1)S(1)}, u32[]{:S(2)}, u32[]{:S(2)}) %all-to-all-start.1) | async-done | bytes 1310752 | tf_op jit(solution)/shard_map/all_to_all | solution.py:218
  578.2 1.4 copy.111
  (126 shorter events, 39.4 us)
Async XLA Ops:
  7.2 14.2 %copy-start = (s32[32]{0:T(128)S(1)}, s32[32]{0:T(128)}, u32[]{:S(2)}) copy-start(s32[32]{0:T(128)} %param.20) | copy-start | bytes 388
  7.2 15.5 %copy-start.16 = (f32[128]{0:T(128)S(1)}, f32[128]{0:T(128)}, u32[]{:S(2)}) copy-start(f32[128]{0:T(128)} %param.16) | copy-start | bytes 1540
  7.2 15.5 %copy-start.17 = (f32[128]{0:T(128)S(1)}, f32[128]{0:T(128)}, u32[]{:S(2)}) copy-start(f32[128]{0:T(128)} %param.17) | copy-start | bytes 1540
  7.2 15.5 %copy-start.4 = (bf16[128,2560]{1,0:T(8,128)(2,1)S(1)}, bf16[128,2560]{1,0:T(8,128)(2,1)}, u32[]{:S(2)}) copy-start(bf16[128,2560]{1,0:T(8,128)(2,1)} %param.15) | copy-start | bytes 1966084
  7.2 90.3 %all-gather.4.cloned.1.call-start = ((), (), s32[]{:S(2)}) async-start(), calls=%async_computation.9 | async-start | bytes 4456448 | tf_op jit(solution)/shard_map/all_gather | solution.py:35
  14.9 232.3 %reduce-scatter.3.cloned.1.call-start = ((), (), s32[]{:S(2)}) async-start(), calls=%async_computation.7 | async-start | bytes 4456448 | tf_op jit(solution)/shard_map/reduce_scatter | solution.py:52
  102.9 1.3 copy-start.10
  104.9 0.9 copy-start.11
  106.6 0.9 copy-start.12
  108.2 0.9 copy-start.13
  117.4 1.2 copy-start.6
  121.0 0.9 copy-start.8
  122.7 0.9 copy-start.9
  132.6 1.3 copy-start.3
  135.3 111.9 %all-to-all-start.2 = ((bf16[128,32,160]{0,2,1:T(8,128)(2,1)}), bf16[128,32,160]{0,2,1:T(8,128)(2,1)S(1)}, u32[]{:S(2)}, u32[]{:S(2)}) async-start(bf16[128,32,160]{0,2,1:T(8,128)(2,1)} %bitcast.50), calls=%async_computation.4 | async-start | bytes 2621440 | tf_op jit(solution)/shard_map/all_to_all | solution.py:187
  144.3 126.9 %reduce-scatter.5.cloned.1.call-start = ((), (), s32[]{:S(2)}) async-start(), calls=%async_computation.8 | async-start | bytes 393216 | tf_op jit(solution)/shard_map/reduce_scatter | solution.py:52
  474.5 1.9 copy-start.2
  476.4 18.0 %copy-start.5 = (bf16[160,512]{1,0:T(8,128)(2,1)S(1)}, bf16[160,512]{1,0:T(8,128)(2,1)}, u32[]{:S(2)}) copy-start(bf16[160,512]{1,0:T(8,128)(2,1)} %param.21) | copy-start | bytes 491524
  476.4 18.0 %copy-start.14 = (bf16[10,512]{1,0:T(8,128)(2,1)S(1)}, bf16[10,512]{1,0:T(8,128)(2,1)}, u32[]{:S(2)}) copy-start(bf16[10,512]{1,0:T(8,128)(2,1)} %param.23) | copy-start | bytes 30724
  476.4 18.0 %copy-start.15 = (bf16[10,512]{1,0:T(8,128)(2,1)S(1)}, bf16[10,512]{1,0:T(8,128)(2,1)}, u32[]{:S(2)}) copy-start(bf16[10,512]{1,0:T(8,128)(2,1)} %param.22) | copy-start | bytes 30724
  478.0 16.4 %all-to-all-start.3 = ((bf16[16,10,512]{2,1,0:T(8,128)(2,1)}), bf16[16,10,512]{2,1,0:T(8,128)(2,1)S(1)}, u32[]{:S(2)}, u32[]{:S(2)}) async-start(bf16[16,10,512]{2,1,0:T(8,128)(2,1)} %reshape.271), calls=%async_computation.5 | async-start | bytes 524288 | tf_op jit(solution)/shard_map/all_to_all | solution.py:68
  495.8 13.1 %all-to-all-start.4 = ((bf16[16,10,512]{2,1,0:T(8,128)(2,1)}), bf16[16,10,512]{2,1,0:T(8,128)(2,1)S(1)}, u32[]{:S(2)}, u32[]{:S(2)}) async-start(bf16[16,10,512]{2,1,0:T(8,128)(2,1)} %broadcast_in_dim.19), calls=%async_computation.6 | async-start | bytes 524288 | tf_op jit(solution)/shard_map/all_to_all | solution.py:74
  508.9 70.8 %copy-start.1 = (s32[32]{0:T(128)S(1)}, s32[32]{0:T(128)}, u32[]{:S(2)}) copy-start(s32[32]{0:T(128)} %param.20) | copy-start | bytes 388
  508.9 69.3 %all-to-all-start.1 = ((bf16[32,128,160]{1,2,0:T(8,128)(2,1)}), bf16[32,128,160]{1,2,0:T(8,128)(2,1)S(1)}, u32[]{:S(2)}, u32[]{:S(2)}) async-start(bf16[32,128,160]{1,2,0:T(8,128)(2,1)} %bitcast.96), calls=%async_computation.3 | async-start | bytes 2621440 | tf_op jit(solution)/shard_map/all_to_all | solution.py:218
  (1 other events, 0.9 us)
Sparse Core Ops, SparseCore 0:
  15.0 82.4 all-gather.3
  132.7 114.4 reduce-scatter.2
  250.0 21.1 reduce-scatter.4
